TPU v7x, 32 devices: a whole 2x2x4 slice. The times are simulated.
32 devices in a mesh: groups: 1, dom: 4 (over z), cls: 4 (over y, x), pix: 2 (over core).
Axes of the slice: x: 2, y: 2, z: 4, core: 2. Of those that a mesh axis runs over, the one named last changes fastest.
Arguments:
- particles: float32 [512, 2, 4096], P(('groups', 'dom', 'cls', 'pix')), may hold values from -10 to 10
- templates: bfloat16 [100, 2, 4096], P(('groups', 'cls')), may hold values from -0.5 to 0.5
- offsets: int32 [9, 2], replicated, may hold values from -3 to 3, as said below
- micrograph: int32 [512], P(('groups', 'dom', 'cls', 'pix')), may hold values from 0 to 63
- noise_var: float32 [64], P('groups'), may hold values from 0.25 to 2
- prior_rot: int32 [512], P(('groups', 'dom', 'cls', 'pix')), may hold values from 0 to 3
- earlier_class_labels: int32 [512], P(('groups', 'dom', 'cls', 'pix')), may hold values from 0 to 99
Outputs:
- class_sums: float32 [100, 2, 4096], P(('groups', 'cls'), None, ('dom', 'pix'))
- class_weights: float32 [100], P(('groups', 'cls'))
- log_evidence: float32 [1], P('groups')
Inputs may be any that keep to these rules, and one draw needn't show every extreme that they name: 9 distinct offsets on the 7 x 7 grid of whole-pixel shifts, with (-3, -3) and (3, 3) among them.
All inputs are finite; a program needn't handle non-finite values.
Results may differ from a plain program's by a relative error of at most 0.008.
Values may be sent and summed in bfloat16 or wider, within the bound.
A program may use at most 192 MiB of HBM per device.

v0:
```python
import math

import jax
import jax.numpy as jnp
from jax import lax
from jax.sharding import PartitionSpec as P

RAD = 32
ANG = 128
CLASS_COUNT = 100
ROT = 4


KAPPA = 2.0
PRIOR_REWARD = 1.5
MOVE_WEIGHT = 0.125


def shifted_images(particles, offsets):
    radius = jnp.arange(RAD, dtype=jnp.float32) + 1.0
    angle_grid = 2.0 * math.pi / ANG * jnp.arange(ANG, dtype=jnp.float32)
    wave_first = (radius[:, None] * jnp.cos(angle_grid)[None, :]).reshape(-1)
    wave_second = (radius[:, None] * jnp.sin(angle_grid)[None, :]).reshape(-1)
    offset_first = offsets[:, 0].astype(jnp.float32)
    offset_second = offsets[:, 1].astype(jnp.float32)
    phase_table = (
        2.0
        * math.pi
        / (2 * RAD)
        * (
            offset_first[:, None] * wave_first[None, :]
            + offset_second[:, None] * wave_second[None, :]
        )
    )
    cosine = jnp.cos(phase_table)[None]
    sine_part = jnp.sin(phase_table)[None]
    real_part = particles[:, 0, :][:, None, :]
    imag_part = particles[:, 1, :][:, None, :]
    new_real = real_part * cosine + imag_part * sine_part
    new_imag = imag_part * cosine - real_part * sine_part
    return jnp.stack([new_real, new_imag], axis=2).astype(jnp.bfloat16)


def row_terms(micrograph, prior_rot, earlier_class_labels, noise_var, offsets):
    inverse = jnp.sum(
        jnp.where(
            micrograph[:, None] == jnp.arange(noise_var.shape[0], dtype=jnp.int32)[None, :],
            1.0 / noise_var[None, :],
            0.0,
        ),
        axis=1,
    )
    turn_prior = KAPPA * jnp.cos(
        2.0
        * math.pi
        / ROT
        * (jnp.arange(ROT, dtype=jnp.int32)[:, None] - prior_rot[None, :]).astype(jnp.float32)
    )
    class_agreement = jnp.where(
        jnp.arange(CLASS_COUNT, dtype=jnp.int32)[:, None] == earlier_class_labels[None, :],
        PRIOR_REWARD,
        0.0,
    )
    offset_first = offsets[:, 0].astype(jnp.float32)
    offset_second = offsets[:, 1].astype(jnp.float32)
    move_prior = -MOVE_WEIGHT * (offset_first * offset_first + offset_second * offset_second)
    return (inverse, turn_prior, class_agreement, move_prior)


def rotate_block(block_tmpl, first_rot, group_size):
    size_block = block_tmpl.shape[0]
    polar_grid = block_tmpl.reshape(size_block, 2, RAD, ANG)
    doubled = jnp.concatenate([polar_grid, polar_grid], axis=3)
    step_size = ANG // ROT
    pieces = [
        lax.dynamic_slice_in_dim(doubled, ANG - (first_rot + within) * step_size, ANG, 3)
        for within in range(group_size)
    ]
    return jnp.stack(pieces, axis=0).reshape(group_size * size_block, 2 * RAD * ANG)


def block_energy(block_tmpl):
    widened = block_tmpl.astype(jnp.float32)
    return jnp.sum(widened * widened, axis=(1, 2))


def split_features(sum_store):
    return lax.psum_scatter(sum_store, ("dom", "pix"), scatter_dimension=2, tiled=True)


def body(particles, templates, offsets, micrograph, noise_var, prior_rot, earlier_class_labels):
    particle_count = particles.shape[0]
    size_block = templates.shape[0]
    shift_count = offsets.shape[0]
    cls_size = lax.axis_size("cls")
    cls_index = lax.axis_index("cls")
    total_particles = particle_count * lax.axis_size("dom") * cls_size * lax.axis_size("pix")
    group_size = math.gcd(ROT, 4)
    group_count = ROT // group_size
    step_size = ANG // ROT
    feature_count = RAD * ANG
    kept_shape = (group_count, group_size, size_block, particle_count, shift_count)

    def scores(block_tmpl, energy, first_class, first_rot, images_flat, row_extras):
        inverse, turn_prior, class_agreement, move_prior = row_extras
        rotated = rotate_block(block_tmpl, first_rot, group_size)
        correlation = lax.dot_general(
            rotated, images_flat, (((1,), (1,)), ((), ())), preferred_element_type=jnp.float32
        )
        correlation = correlation.reshape(group_size, size_block, particle_count, shift_count)
        match_part = lax.dynamic_slice_in_dim(class_agreement, first_class, size_block, 0)
        return (
            (correlation - 0.5 * energy[None, :, None, None]) * inverse[None, None, :, None]
            + move_prior[None, None, None, :]
            + turn_prior[:, None, :, None]
            + match_part[None, :, :, None]
        )

    def normalize_block(block_tmpl, first_class, images_flat, row_extras, loop_state):
        energy = block_energy(block_tmpl)

        def normalize_group_turn(group_index, inner_state):
            highest, running_sum, kept = inner_state
            values = scores(
                block_tmpl, energy, first_class, group_index * group_size, images_flat, row_extras
            )
            new_high = jnp.maximum(highest, jnp.max(values, axis=(0, 1, 3)))
            running_sum = running_sum * jnp.exp(highest - new_high) + jnp.sum(
                jnp.exp(values - new_high[None, None, :, None]), axis=(0, 1, 3)
            )
            kept = lax.dynamic_update_index_in_dim(kept, values, group_index, 0)
            return (new_high, running_sum, kept)

        initial = (loop_state[0], loop_state[1], jnp.zeros(kept_shape, jnp.float32))
        return lax.fori_loop(0, group_count, normalize_group_turn, initial)

    def collect_block(kept, images_flat, evidence):

        def collect_group_turn(group_index, inner_state):
            block_sum, block_weight = inner_state
            first_rot = group_index * group_size
            values = lax.dynamic_index_in_dim(kept, group_index, 0, keepdims=False)
            posterior = jnp.exp(values - evidence[None, None, :, None]).astype(jnp.bfloat16)
            block_weight = block_weight + jnp.sum(posterior.astype(jnp.float32), axis=(0, 2, 3))
            aligned = jnp.dot(
                posterior.reshape(group_size * size_block, particle_count * shift_count),
                images_flat,
                preferred_element_type=jnp.float32,
            )
            aligned = aligned.reshape(group_size, size_block, 2, RAD, ANG)
            doubled = jnp.concatenate([aligned, aligned], axis=4)
            for within in range(group_size):
                block_sum = block_sum + lax.dynamic_slice_in_dim(
                    doubled[within], (first_rot + within) * step_size, ANG, 3
                )
            return (block_sum, block_weight)

        initial = (
            jnp.zeros((size_block, 2, RAD, ANG), jnp.float32),
            jnp.zeros((size_block,), jnp.float32),
        )
        block_sum, block_weight = lax.fori_loop(0, group_count, collect_group_turn, initial)
        return (block_sum.reshape(size_block, 2, feature_count), block_weight)

    own_first = cls_index * size_block
    all_kept = jnp.zeros((cls_size,) + kept_shape, jnp.float32)
    prepare_images_flat = shifted_images(particles, offsets).reshape(
        particles.shape[0] * shift_count, 2 * feature_count
    )
    prepare_row_extras = row_terms(micrograph, prior_rot, earlier_class_labels, noise_var, offsets)
    images_flat = prepare_images_flat
    row_extras = prepare_row_extras
    held_block = lax.all_gather(templates, "cls", axis=0, tiled=True)

    def current_block(held_now, owner_index):
        return lax.dynamic_slice_in_dim(held_now, owner_index * size_block, size_block, 0)

    def first_turn(turn_index, outer_state):
        held_now, highest, running_sum, retained_entries = outer_state
        owner_index = (cls_index - turn_index) % cls_size
        highest, running_sum, kept = normalize_block(
            current_block(held_now, owner_index),
            owner_index * size_block,
            images_flat,
            row_extras,
            (highest, running_sum),
        )
        retained_entries = lax.dynamic_update_index_in_dim(retained_entries, kept, turn_index, 0)
        return (held_now, highest, running_sum, retained_entries)

    highest, running_sum = (
        jnp.full((particle_count,), -jnp.inf, jnp.float32),
        jnp.zeros((particle_count,), jnp.float32),
    )
    held_block, highest, running_sum, all_kept = lax.fori_loop(
        0, cls_size, first_turn, (held_block, highest, running_sum, all_kept)
    )
    evidence = highest + jnp.log(running_sum)

    def second_turn(turn_index, outer_state):
        sum_store, weights_all = outer_state
        owner_index = (cls_index - turn_index) % cls_size
        kept = lax.dynamic_index_in_dim(all_kept, turn_index, 0, keepdims=False)
        block_sum, block_weight = collect_block(kept, images_flat, evidence)
        weights_all = lax.dynamic_update_slice_in_dim(
            weights_all, block_weight, owner_index * size_block, 0
        )
        sum_store = lax.dynamic_update_slice_in_dim(
            sum_store, block_sum, owner_index * size_block, 0
        )
        return (sum_store, weights_all)

    store_rows = CLASS_COUNT
    initial = (
        jnp.zeros((store_rows, 2, feature_count), jnp.float32),
        jnp.zeros((CLASS_COUNT,), jnp.float32),
    )
    sum_store, weights_all = lax.fori_loop(0, cls_size, second_turn, initial)
    local_evidence = jnp.sum(evidence)
    sum_store = lax.psum_scatter(sum_store, "cls", scatter_dimension=0, tiled=True)
    class_sums = split_features(sum_store)
    weight_total, summed_evidence = lax.psum(
        (weights_all, local_evidence[None]), ("dom", "cls", "pix")
    )
    class_weights = lax.dynamic_slice_in_dim(weight_total, own_first, size_block, 0)
    log_evidence = summed_evidence / total_particles
    return (class_sums, class_weights, log_evidence)


def solution(mesh):
    in_specs = (
        P(("groups", "dom", "cls", "pix"), None, None),
        P(("groups", "cls"), None, None),
        P(),
        P(("groups", "dom", "cls", "pix")),
        P("groups"),
        P(("groups", "dom", "cls", "pix")),
        P(("groups", "dom", "cls", "pix")),
    )
    out_specs = (P(("groups", "cls"), None, ("dom", "pix")), P(("groups", "cls")), P("groups"))
    return jax.shard_map(body, mesh=mesh, in_specs=in_specs, out_specs=out_specs, check_vma=False)
```

profile of v0, /device:TPU:0, one launch (start us, length us, event | category | flops | bytes accessed | tf_op | source)
XLA Modules:
  0.0 394.9 jit_solution(2151171327407519790)
XLA Ops:
  8.8 1.7 fusion.45
  12.0 4.9 %add_convert_fusion = (bf16[16,9,1,4096]{3,2,1,0:T(2,128)(2,1)S(1)}, bf16[16,9,1,4096]{3,2,1,0:T(2,128)(2,1)S(1)}) fusion(f32[9,4096]{1,0:T(8,128)S(1)} %get-tuple-element.780, f32[16,4096]{1,0:T(8,128)S(1)} %get-tuple-element.787, f32[9,4096]{1,0:T(8,128)S(1)} %get-tuple-element.779, f32[16,4096]{1,0:T(8,128)S(1)} %get-tuple-element.788), kind=kLoop, calls=%fused_computation.48 | loop fusion | flops 4718592 | bytes 3178496 | tf_op jit(solution)/shard_map/convert
  16.9 5.3 %pad_maximum_fusion.1 = bf16[16,9,2,4096]{3,2,1,0:T(2,128)(2,1)S(1)} fusion(bf16[16,9,1,4096]{3,2,1,0:T(2,128)(2,1)S(1)} %get-tuple-element.776, bf16[16,9,1,4096]{3,2,1,0:T(2,128)(2,1)S(1)} %get-tuple-element.775), kind=kLoop, calls=%fused_computation.46 | loop fusion | flops 4718592 | bytes 4718592 | tf_op jit(solution)/shard_map/stack | solution.py:41
  22.3 1.5 copy.44
  24.1 20.0 %all-gather.2.cloned.1.call-done = bf16[100,2,4096]{2,1,0:T(2,128)(2,1)} async-done(((bf16[25,2,4096]{2,1,0:T(2,128)(2,1)}), bf16[100,2,4096]{2,1,0:T(2,128)(2,1)}) %all-gather.2.cloned.1.call-update) | async-done | bytes 1638416 | tf_op jit(solution)/shard_map/all_gather | solution.py:173
  44.1 68.0 %while.67 = (s32[]{:T(128)}, f32[16]{0:T(128)S(1)}, f32[16]{0:T(128)S(1)}, f32[4,1,4,25,16,9]{3,4,5,2,1,0:T(8,128)}, s32[]{:T(128)}, /*index=5*/bf16[100,2,4096]...) while((s32[]{:T(128)}, f32[16]{0:T(128)S(1)}, ...), condition=%wide.region_5.6_spmd.clone, body=%wide.region_1.5_spmd.clone.sunk | while | flops 243213152 | bytes 21479116 | solution.py:195
  44.2 2.0 multiply_reduce_fusion.2
  48.9 2.0 stack.61
  53.0 2.5 dot_general.21
  55.5 4.5 %fusion.59 = (f32[16]{0:T(128)S(1)}, f32[4,25,16,9]{1,2,3,0:T(8,128)S(1)}) fusion(f32[25,16]{0,1:T(8,128)S(1)} %constant_dynamic-slice_fusion.8, f32[4,16]{1,0:T(4,128)S(1)} %cosine_multiply_fusion.2, f32[9]{0:T(128)S(1)} %get-tuple-element.955, f32[16]{0:T(128)S(1)} %get-tuple-element.954, f32[25]{0:T(128)S(1)} %broadcast_multiply_fusion.2, ...), kind=kOutput, calls=%fused_computation.72.clone.1 | convolution fusion | flops 242569584 | bytes 4057416 | tf_op jit(solution)/shard_map/while/body/eval_jaxpr/while/body/eval_jaxpr/dot_general | solution.py:107
  61.2 2.0 multiply_reduce_fusion.2
  64.8 1.1 fusion.58
  65.9 2.0 stack.61
  70.1 2.5 dot_general.21
  72.6 4.5 %fusion.59 = (f32[16]{0:T(128)S(1)}, f32[4,25,16,9]{1,2,3,0:T(8,128)S(1)}) fusion(f32[25,16]{0,1:T(8,128)S(1)} %constant_dynamic-slice_fusion.8, f32[4,16]{1,0:T(4,128)S(1)} %cosine_multiply_fusion.2, f32[9]{0:T(128)S(1)} %get-tuple-element.955, f32[16]{0:T(128)S(1)} %get-tuple-element.954, f32[25]{0:T(128)S(1)} %broadcast_multiply_fusion.2, ...), kind=kOutput, calls=%fused_computation.72.clone.1 | convolution fusion | flops 242569584 | bytes 4057416 | tf_op jit(solution)/shard_map/while/body/eval_jaxpr/while/body/eval_jaxpr/dot_general | solution.py:107
  78.2 2.0 multiply_reduce_fusion.2
  82.9 2.0 stack.61
  87.1 2.5 dot_general.21
  89.6 4.5 %fusion.59 = (f32[16]{0:T(128)S(1)}, f32[4,25,16,9]{1,2,3,0:T(8,128)S(1)}) fusion(f32[25,16]{0,1:T(8,128)S(1)} %constant_dynamic-slice_fusion.8, f32[4,16]{1,0:T(4,128)S(1)} %cosine_multiply_fusion.2, f32[9]{0:T(128)S(1)} %get-tuple-element.955, f32[16]{0:T(128)S(1)} %get-tuple-element.954, f32[25]{0:T(128)S(1)} %broadcast_multiply_fusion.2, ...), kind=kOutput, calls=%fused_computation.72.clone.1 | convolution fusion | flops 242569584 | bytes 4057416 | tf_op jit(solution)/shard_map/while/body/eval_jaxpr/while/body/eval_jaxpr/dot_general | solution.py:107
  95.2 2.0 multiply_reduce_fusion.2
  99.9 2.0 stack.61
  104.1 2.5 dot_general.21
  106.6 4.5 %fusion.59 = (f32[16]{0:T(128)S(1)}, f32[4,25,16,9]{1,2,3,0:T(8,128)S(1)}) fusion(f32[25,16]{0,1:T(8,128)S(1)} %constant_dynamic-slice_fusion.8, f32[4,16]{1,0:T(4,128)S(1)} %cosine_multiply_fusion.2, f32[9]{0:T(128)S(1)} %get-tuple-element.955, f32[16]{0:T(128)S(1)} %get-tuple-element.954, f32[25]{0:T(128)S(1)} %broadcast_multiply_fusion.2, ...), kind=kOutput, calls=%fused_computation.72.clone.1 | convolution fusion | flops 242569584 | bytes 4057416 | tf_op jit(solution)/shard_map/while/body/eval_jaxpr/while/body/eval_jaxpr/dot_general | solution.py:107
  112.7 3.4 broadcast_in_dim.92
  116.1 39.7 %while.66 = (s32[]{:T(128)}, f32[100,2,4096]{2,1,0:T(2,128)}, f32[100]{0:T(128)S(1)}, f32[4,1,4,25,16,9]{3,4,5,2,1,0:T(8,128)}, f32[16]{0:T(128)S(1)}, /*index=5...) while((s32[]{:T(128)}, f32[100,2,4096]{2,1,0:T(2,128)}, ...), condition=%wide.region_8.9_spmd, body=%wide.region_6.8_spmd.sunk | while | flops 237244768 | bytes 21620700 | solution.py:218
  118.5 1.8 fusion.56
  120.3 1.7 fusion.57
  122.5 1.3 add.485
  123.8 2.1 constant_dynamic-update-slice_fusion.6
  128.4 1.8 fusion.56
  130.2 1.7 fusion.57
  132.4 1.3 add.485
  133.8 2.1 constant_dynamic-update-slice_fusion.6
  138.3 1.8 fusion.56
  140.2 1.7 fusion.57
  142.3 1.3 add.485
  143.7 2.2 constant_dynamic-update-slice_fusion.6
  148.3 1.8 fusion.56
  150.1 1.7 fusion.57
  152.3 1.3 add.485
  153.6 2.1 constant_dynamic-update-slice_fusion.6
  157.6 87.7 %all-reduce.4.cloned.1.call-done = f32[100,2,4096]{2,1,0:T(2,128)} async-done(((f32[100,2,4096]{2,1,0:T(2,128)}), f32[100,2,4096]{2,1,0:T(2,128)}) %all-reduce.4.cloned.1.call-update) | async-done | bytes 3276816
  245.3 1.2 constant_dynamic-slice_fusion.3
  246.5 34.3 %copy.38 = f32[25,2,4096]{1,0,2:T(8,128)} copy(f32[25,2,4096]{2,1,0:T(2,128)S(1)} %constant_dynamic-slice_fusion.3) | data formatting | bytes 1638400
  280.8 49.2 %reshape.339 = f32[4096,50]{1,0:T(8,128)} reshape(f32[4096,25,2]{2,1,0:T(8,128)} %bitcast.17) | data formatting | bytes 1638400
  330.1 40.4 %all-reduce.1 = (f32[100]{0:T(128)S(1)}, f32[1]{0:T(128)}) all-reduce(f32[100]{0:T(128)S(1)} %get-tuple-element.660, f32[1]{0:T(128)} %bitcast.12), channel_id=1, replica_groups=mesh['groups'=1,'dom'=4,'cls'=4,'pix'=2] {'dom','cls','pix'}, use_global_device_ids=true, to_apply=%region_11.12 | all-reduce | flops 101 | bytes 808 | tf_op jit(solution)/shard_map/psum | solution.py:222
  371.8 9.0 %reshape.340 = f32[512,25,2]{2,1,0:T(8,128)} reshape(f32[512,50]{1,0:T(8,128)} %reduce-scatter.4.cloned.1.call-done) | data formatting | bytes 204800
  380.8 6.5 %copy.39 = f32[25,2,512]{2,1,0:T(2,128)} copy(f32[25,2,512]{1,0,2:T(8,128)} %bitcast.102) | data formatting | bytes 204800
  (135 shorter events, 40.0 us)
Async XLA Ops:
  7.2 36.9 %all-gather.2.cloned.1.call-start = ((), (), s32[]{:S(2)}) async-start(), calls=%async_computation.1 | async-start | bytes 2048000 | tf_op jit(solution)/shard_map/all_gather | solution.py:173
  7.9 237.4 %all-reduce.4.cloned.1.call-start = ((), (), s32[]{:S(2)}) async-start(), calls=%async_computation.3 | async-start | bytes 6553600
  22.3 1.6 copy-start.5
  22.3 1.6 copy-start.6
  22.3 1.8 copy-start.3
  22.3 1.8 copy-start.4
  22.3 21.8 %copy-start.2 = (s32[16]{0:T(128)S(1)}, s32[16]{0:T(128)}, u32[]{:S(2)}) copy-start(s32[16]{0:T(128)} %param.16) | copy-start | bytes 196
  53.0 2.5 copy-start
  53.0 2.5 copy-start.1
  70.1 2.5 copy-start
  70.1 2.5 copy-start.1
  87.1 2.5 copy-start
  87.1 2.5 copy-start.1
  104.1 2.5 copy-start
  104.1 2.5 copy-start.1
  155.7 0.7 copy-start.7
  155.8 216.0 %reduce-scatter.4.cloned.1.call-start = ((), (), s32[]{:S(2)}) async-start(), calls=%async_computation.2 | async-start | bytes 2359296
Sparse Core Ops, SparseCore 0:
  9.8 34.2 all-gather.1
  155.9 89.3 all-reduce.3
  330.2 35.8 reduce-scatter.3
where the time goes:
time: 397 us; the launch traced here: 395 us
  local copies, waits for them, and re-layouts  173 us (44%)
  waiting for transfers between devices  108 us (27%)
  blocking collectives  40.4 us (10%)
  other arithmetic  31.3 us (8%)
  matrix products  25.3 us (6%)
  between operations  16.4 us (4%)
    unnamed x19, local copies, waits for them, and re-layouts  103 us
    unnamed x5, waiting for transfers between devices  88.4 us
    psum x1, blocking collectives, body(): lax.psum((weights_all, local_evidence[None]), ('dom', 'cls', 'pix'))  40.4 us
    another operation x16, local copies, waits for them, and re-layouts, rotate_block(): jnp.stack(pieces, axis=0).reshape(group_size * size_block, 2 * RAD * ANG)  20.6 us
    all_gather x1, waiting for transfers between devices, body(): held_block = lax.all_gather(templates, 'cls', axis=0, tiled=True)  20 us
    dot_general x4, matrix products, scores(): lax.dot_general(rotated, images_flat, (((1,), (1,)), ((), ())), preferred...  18.1 us
    dot_general x4, local copies, waits for them, and re-layouts, scores(): lax.dot_general(rotated, images_flat, (((1,), (1,)), ((), ())), preferred...  9.98 us
    dynamic_update_slice x4, local copies, waits for them, and re-layouts, second_turn(): lax.dynamic_update_slice_in_dim(sum_store, block_sum, owner_index * size_...  8.55 us
  transfers between devices with their start and end apart: 3, of which 2 were waited for; matrix products, arithmetic and copies ran while one was open for 4% of the time, Pallas kernels for 0%

commit v1 on v0

--- a/solution.py
+++ b/solution.py
@@ -1,8 +1,12 @@
+import functools
 import math
 
 import jax
 import jax.numpy as jnp
+import numpy as np
 from jax import lax
+from jax.experimental import pallas as pl
+from jax.experimental.pallas import tpu as pltpu
 from jax.sharding import PartitionSpec as P
 
 RAD = 32
@@ -227,6 +231,283 @@
     return (class_sums, class_weights, log_evidence)
 
 
+AXES = ("groups", "dom", "cls", "pix")
+PAD = 32
+
+
+def wave_tables():
+    radius = np.arange(RAD) + 1.0
+    angle = 2.0 * np.pi / ANG * np.arange(ANG)
+    first = (radius[:, None] * np.cos(angle)[None, :]).reshape(-1) * (2.0 * np.pi / (2 * RAD))
+    second = (radius[:, None] * np.sin(angle)[None, :]).reshape(-1) * (2.0 * np.pi / (2 * RAD))
+    rows = [np.cos(first), np.sin(first), np.cos(second), np.sin(second)]
+    return np.stack(rows + rows).astype(np.float32)
+
+
+def powers(cosine, sine_part, amount):
+    c2, s2 = cosine * cosine - sine_part * sine_part, 2.0 * cosine * sine_part
+    c3, s3 = c2 * cosine - s2 * sine_part, s2 * cosine + c2 * sine_part
+    size = jnp.abs(amount)
+    c = jnp.where(size < 0.5, 1.0, jnp.where(size < 1.5, cosine, jnp.where(size < 2.5, c2, c3)))
+    s = jnp.where(size < 0.5, 0.0, jnp.where(size < 1.5, sine_part, jnp.where(size < 2.5, s2, s3)))
+    return c, jnp.where(amount < 0.0, -s, s)
+
+
+def fused(
+    dims, part_ref, tmpl_ref, wave_ref, ext_ref, out_ref, small_ref,
+    held, images, corr, total, sib_out, sib_in, cls_out, cls_in, dom_out, dom_in, small_in,
+    own_sem, gather_s, gather_r, forward_s, forward_r, sib_s, sib_r, cls_s, cls_r,
+    dom_s, dom_r, small_s, small_r, small_a, small_b, small_c,
+):
+    doms, clss, count, shifts, chunk = dims
+    group, dom = lax.axis_index("groups"), lax.axis_index("dom")
+    cls, pix = lax.axis_index("cls"), lax.axis_index("pix")
+    other = 1 - pix
+    sibling = (group, dom, cls, other)
+    cls_peers = [(group, dom, lax.rem(cls + k, clss), pix) for k in range(1, clss)]
+    dom_peers = [(group, lax.rem(dom + k, doms), cls, pix) for k in range(1, doms)]
+    mesh_id = pl.DeviceIdType.MESH
+
+    def send(src, dst, s, r, target):
+        copy = pltpu.make_async_remote_copy(
+            src_ref=src, dst_ref=dst, send_sem=s, recv_sem=r,
+            device_id=target, device_id_type=mesh_id,
+        )
+        copy.start()
+        return copy
+
+    barrier = pltpu.get_barrier_semaphore()
+    for target in [sibling] + cls_peers + dom_peers:
+        pl.semaphore_signal(barrier, inc=1, device_id=target, device_id_type=mesh_id)
+    pl.semaphore_wait(barrier, clss + doms - 1)
+
+    pending = []
+    gathers = [
+        send(tmpl_ref.at[pix], held.at[pix, cls], gather_s.at[k], gather_r.at[k], target)
+        for k, target in enumerate(cls_peers)
+    ]
+    own_copies = [
+        pltpu.make_async_copy(tmpl_ref.at[c], held.at[c, cls], own_sem.at[c]) for c in range(2)
+    ]
+    for copy in own_copies:
+        copy.start()
+
+    step_size = ANG // ROT
+    per_rot = shifts * count
+    move_x = ext_ref[:, 40:41] + jnp.zeros((count, ANG), jnp.float32)
+    move_y = ext_ref[:, 41:42] + jnp.zeros((count, ANG), jnp.float32)
+
+    def make_images(g, carry):
+        lanes = pl.ds(pl.multiple_of(g * ANG, ANG), ANG)
+        waves = wave_ref[:, lanes]
+        cx, sx = powers(waves[0:1], waves[1:2], move_x)
+        cy, sy = powers(waves[2:3], waves[3:4], move_y)
+        cosine = cx * cy - sx * sy
+        sine_part = sx * cy + cx * sy
+        real, imag = part_ref[0, :, lanes], part_ref[1, :, lanes]
+        for rot in range(ROT):
+            if rot:
+                turn = ANG - rot * step_size
+                co, si = pltpu.roll(cosine, turn, 1), pltpu.roll(sine_part, turn, 1)
+                re, im = pltpu.roll(real, turn, 1), pltpu.roll(imag, turn, 1)
+            else:
+                co, si, re, im = cosine, sine_part, real, imag
+            for t in range(shifts):
+                c, s = co[t : t + 1], si[t : t + 1]
+                row = rot * per_rot + t * count
+                images[0, row : row + count, lanes] = (re * c + im * s).astype(jnp.bfloat16)
+                images[1, row : row + count, lanes] = (im * c - re * s).astype(jnp.bfloat16)
+        return carry
+
+    lax.fori_loop(0, RAD, make_images, 0)
+
+    forwards = []
+    for k, copy in enumerate(gathers):
+        copy.wait_recv()
+        owner = lax.rem(cls + clss - 1 - k, clss)
+        forwards.append(
+            send(held.at[pix, owner], held.at[pix, owner], forward_s.at[k], forward_r.at[k], sibling)
+        )
+    for copy in own_copies:
+        copy.wait()
+
+    piece = 512
+    corr[...] = jnp.zeros_like(corr)
+
+    def correlate(comp):
+        def step(n, energy):
+            lanes = pl.ds(pl.multiple_of(n * piece, piece), piece)
+            tmpl = held[comp, :, :, lanes].reshape(clss * PAD, piece)
+            corr[...] += lax.dot_general(
+                tmpl, images[comp, :, lanes], (((1,), (1,)), ((), ())),
+                preferred_element_type=jnp.float32,
+            )
+            wide = tmpl.astype(jnp.float32)
+            wide = wide * wide
+            for q in range(piece // ANG):
+                energy = energy + wide[:, q * ANG : (q + 1) * ANG]
+            return energy
+        return step
+
+    energy = jnp.zeros((clss * PAD, ANG), jnp.float32)
+    energy = lax.fori_loop(0, RAD * ANG // piece, correlate(pix), energy)
+    for copy in forwards:
+        copy.wait_recv()
+    energy = lax.fori_loop(0, RAD * ANG // piece, correlate(other), energy)
+    energy = jnp.sum(energy, axis=1, keepdims=True)
+
+    turned = jnp.transpose(corr[...] - 0.5 * energy).reshape(ROT * shifts, count, clss * PAD)
+    slot = lax.broadcasted_iota(jnp.int32, (count, clss * PAD), 1)
+    inverse = ext_ref[:, 0:1]
+    match = jnp.where(slot.astype(jnp.float32) == ext_ref[:, 1:2], PRIOR_REWARD, 0.0)
+    real_class = lax.rem(slot, PAD) < CLASS_COUNT // clss
+    match = jnp.where(real_class, match, -1e30)
+    values = [
+        turned[n] * inverse + (match + ext_ref[:, 2 + n : 3 + n]) for n in range(ROT * shifts)
+    ]
+    highest = functools.reduce(jnp.maximum, values)
+    highest = jnp.max(highest, axis=1, keepdims=True)
+    summed = functools.reduce(jnp.add, [jnp.exp(v - highest) for v in values])
+    evidence = highest + jnp.log(jnp.sum(summed, axis=1, keepdims=True))
+    posterior = [
+        jnp.exp(v - evidence).astype(jnp.bfloat16).astype(jnp.float32) for v in values
+    ]
+    weights = jnp.sum(functools.reduce(jnp.add, posterior), axis=0, keepdims=True)
+    evidence_row = jnp.sum(evidence + jnp.zeros((count, clss * PAD), jnp.float32), axis=0, keepdims=True)
+    first_row = lax.broadcasted_iota(jnp.int32, (8, clss * PAD), 0) == 0
+    small_a[...] = jnp.where(first_row, weights, evidence_row)
+    small_sib = send(small_a, small_in.at[0], small_s.at[0], small_r.at[0], sibling)
+    posterior = jnp.transpose(jnp.concatenate(posterior, axis=0)).astype(jnp.bfloat16)
+
+    def block_dot(d, half, comp):
+        lanes = pl.ds(pl.multiple_of((d * 2 + half) * chunk, chunk), chunk)
+        return jnp.dot(
+            posterior, images[comp, :, lanes], preferred_element_type=jnp.float32
+        ).reshape(clss, PAD, chunk)
+
+    order = [lax.rem(dom + j + 1, doms) for j in range(doms)]
+    sib_copies, cls_copies = [], []
+
+    def finish(j):
+        sib_copies[j].wait_recv()
+        for comp in range(2):
+            value = total[j, :, comp] + sib_in[j, :, comp].astype(jnp.float32)
+            total[j, :, comp] = value
+            cls_out[j, :, comp] = value.astype(jnp.bfloat16)
+        cls_copies.append([
+            send(cls_out.at[j, lax.rem(cls + k + 1, clss)], cls_in.at[j, k],
+                 cls_s.at[j, k], cls_r.at[j, k], target)
+            for k, target in enumerate(cls_peers)
+        ])
+
+    for j in range(doms):
+        for comp in range(2):
+            sib_out[j, :, comp] = block_dot(order[j], other, comp).astype(jnp.bfloat16)
+        sib_copies.append(send(sib_out.at[j], sib_in.at[j], sib_s.at[j], sib_r.at[j], sibling))
+        if j:
+            finish(j - 1)
+        for comp in range(2):
+            total[j, :, comp] = block_dot(order[j], pix, comp)
+        if j == 0:
+            small_sib.wait_recv()
+            small_b[...] = small_a[...] + small_in[0]
+            small_cls = [
+                send(small_b, small_in.at[1 + k], small_s.at[1 + k], small_r.at[1 + k], target)
+                for k, target in enumerate(cls_peers)
+            ]
+    finish(doms - 1)
+
+    for copy in small_cls:
+        copy.wait_recv()
+    small_c[...] = functools.reduce(jnp.add, [small_b[...]] + [small_in[1 + k] for k in range(clss - 1)])
+    small_dom = [
+        send(small_c, small_in.at[clss + k], small_s.at[clss + k], small_r.at[clss + k], target)
+        for k, target in enumerate(dom_peers)
+    ]
+
+    dom_copies = []
+    for j in range(doms):
+        for copy in cls_copies[j]:
+            copy.wait_recv()
+        value = total[j, cls]
+        for k in range(clss - 1):
+            value = value + cls_in[j, k].astype(jnp.float32)
+        if j < doms - 1:
+            dom_out[j] = value.astype(jnp.bfloat16)
+            dom_copies.append(
+                send(dom_out.at[j], dom_in.at[j], dom_s.at[j], dom_r.at[j], dom_peers[j])
+            )
+    for j in range(doms - 1):
+        small_dom[j].wait_recv()
+    small_ref[...] = functools.reduce(
+        jnp.add, [small_c[...]] + [small_in[clss + k] for k in range(doms - 1)]
+    )
+    for j in range(doms - 1):
+        dom_copies[j].wait_recv()
+        value = value + dom_in[j].astype(jnp.float32)
+    out_ref[...] = value
+    for copy in gathers + forwards + sib_copies + sum(cls_copies, []) + dom_copies:
+        copy.wait_send()
+    for copy in [small_sib] + small_cls + small_dom:
+        copy.wait_send()
+
+
+def fused_body(doms, clss, particles, templates, offsets, micrograph, noise_var, prior_rot, earlier_class_labels):
+    count, size_block, shifts = particles.shape[0], templates.shape[0], offsets.shape[0]
+    chunk = RAD * ANG // (doms * 2)
+    inverse, turn_prior, _, move_prior = row_terms(
+        micrograph, prior_rot, earlier_class_labels, noise_var, offsets
+    )
+    slots = earlier_class_labels // size_block * PAD + earlier_class_labels % size_block
+    bias = (turn_prior.T[:, :, None] + move_prior[None, None, :]).reshape(count, ROT * shifts)
+    move = jnp.pad(offsets.astype(jnp.float32), ((0, count - shifts), (0, 0)))
+    ext = jnp.concatenate(
+        [inverse[:, None], slots.astype(jnp.float32)[:, None], bias,
+         jnp.zeros((count, 38 - ROT * shifts), jnp.float32), move,
+         jnp.zeros((count, ANG - 42), jnp.float32)], axis=1)
+    tmpl = jnp.pad(jnp.transpose(templates, (1, 0, 2)), ((0, 0), (0, PAD - size_block), (0, 0)))
+    part = jnp.transpose(particles, (1, 0, 2))
+    rows = ROT * shifts * count
+    bf, f32 = jnp.bfloat16, jnp.float32
+    dma = pltpu.SemaphoreType.DMA
+    vmem = pl.BlockSpec(memory_space=pltpu.VMEM)
+    sums, small = pl.pallas_call(
+        functools.partial(fused, (doms, clss, count, shifts, chunk)),
+        out_shape=[
+            jax.ShapeDtypeStruct((2, PAD, chunk), f32),
+            jax.ShapeDtypeStruct((8, clss * PAD), f32),
+        ],
+        in_specs=[vmem] * 4,
+        out_specs=[vmem] * 2,
+        scratch_shapes=[
+            pltpu.VMEM((2, clss, PAD, RAD * ANG), bf),
+            pltpu.VMEM((2, rows, RAD * ANG), bf),
+            pltpu.VMEM((clss * PAD, rows), f32),
+            pltpu.VMEM((doms, clss, 2, PAD, chunk), f32),
+            pltpu.VMEM((doms, clss, 2, PAD, chunk), bf),
+            pltpu.VMEM((doms, clss, 2, PAD, chunk), bf),
+            pltpu.VMEM((doms, clss, 2, PAD, chunk), bf),
+            pltpu.VMEM((doms, clss - 1, 2, PAD, chunk), bf),
+            pltpu.VMEM((doms - 1, 2, PAD, chunk), bf),
+            pltpu.VMEM((doms - 1, 2, PAD, chunk), bf),
+            pltpu.VMEM((clss + doms - 1, 8, clss * PAD), f32),
+            dma((2,)), dma((clss - 1,)), dma((clss - 1,)), dma((clss - 1,)), dma((clss - 1,)),
+            dma((doms,)), dma((doms,)), dma((doms, clss - 1)), dma((doms, clss - 1)),
+            dma((doms - 1,)), dma((doms - 1,)), dma((clss + doms - 1,)), dma((clss + doms - 1,)),
+            pltpu.VMEM((8, clss * PAD), f32),
+            pltpu.VMEM((8, clss * PAD), f32),
+            pltpu.VMEM((8, clss * PAD), f32),
+        ],
+        compiler_params=pltpu.CompilerParams(
+            collective_id=0, has_side_effects=True, vmem_limit_bytes=44 * 2**20
+        ),
+    )(part, tmpl, jnp.asarray(wave_tables()), ext)
+    class_sums = jnp.transpose(sums[:, :size_block], (1, 0, 2))
+    class_weights = lax.dynamic_slice(small[0], (lax.axis_index("cls") * PAD,), (size_block,))
+    log_evidence = small[1, :1] / (count * doms * clss * 2)
+    return class_sums, class_weights, log_evidence
+
+
 def solution(mesh):
     in_specs = (
         P(("groups", "dom", "cls", "pix"), None, None),
@@ -238,4 +519,8 @@
         P(("groups", "dom", "cls", "pix")),
     )
     out_specs = (P(("groups", "cls"), None, ("dom", "pix")), P(("groups", "cls")), P("groups"))
-    return jax.shard_map(body, mesh=mesh, in_specs=in_specs, out_specs=out_specs, check_vma=False)
+    doms, clss = mesh.shape["dom"], mesh.shape["cls"]
+    whole_radii = RAD % (doms * mesh.shape["pix"]) == 0
+    fits = mesh.shape["pix"] == 2 and doms > 1 and clss > 1 and clss * PAD <= ANG
+    chosen = functools.partial(fused_body, doms, clss) if whole_radii and fits else body
+    return jax.shard_map(chosen, mesh=mesh, in_specs=in_specs, out_specs=out_specs, check_vma=False)

time: 397 us -> 51.4 us (0.13)
  local copies, waits for them, and re-layouts: 173 us -> 7.23 us
  waiting for transfers between devices: 108 us -> 0 us
  Pallas kernels: 0 us -> 41 us
  blocking collectives: 40.4 us -> 0 us
  other arithmetic: 31.3 us -> 0.34 us
  matrix products: 25.3 us -> 0 us
  between operations: 16.4 us -> 2.51 us
    unnamed x19 -> x17, local copies, waits for them, and re-layouts: 103 us -> 5.47 us
    unnamed x5 -> x0, waiting for transfers between devices: 88.4 us -> none
    pallas_call x0 -> x1, Pallas kernels: none -> 41 us  [fused_body(): pl.pallas_call(functools.partial(fused, (doms, clss, count, shifts, chunk...]
    psum x1 -> x0, blocking collectives: 40.4 us -> none  [body(): lax.psum((weights_all, local_evidence[None]), ('dom', 'cls', 'pix'))]
    dot_general x8 -> x0, matrix products: 25.3 us -> none  [the longest x4 18.1 us: scores(): lax.dot_general(rotated, images_flat, (((1,), (1,)), ((), ())), preferred...]
    another operation x16 -> x0, local copies, waits for them, and re-layouts: 20.6 us -> none  [rotate_block(): jnp.stack(pieces, axis=0).reshape(group_size * size_block, 2 * RAD * ANG)]
    all_gather x1 -> x0, waiting for transfers between devices: 20 us -> none  [body(): held_block = lax.all_gather(templates, 'cls', axis=0, tiled=True)]
    dynamic_update_slice x12 -> x0, local copies, waits for them, and re-layouts: 12.5 us -> none  [the longest x4 8.55 us: second_turn(): lax.dynamic_update_slice_in_dim(sum_store, block_sum, owner_index * size_...]
  transfers between devices with their start and end apart: 3 -> 0, of which waited for: 2 -> 0; matrix products, arithmetic and copies ran while one was open for 4% -> 0% of each run, Pallas kernels for 0% -> 0%
where the time goes in v1:
time: 51.4 us; the launch traced here: 51.1 us
  Pallas kernels  41 us (80%)
  local copies, waits for them, and re-layouts  7.23 us (14%)
  between operations  2.51 us (5%)
    pallas_call x1, Pallas kernels, fused_body(): pl.pallas_call(functools.partial(fused, (doms, clss, count, shifts, chunk...  41 us
    unnamed x17, local copies, waits for them, and re-layouts  5.47 us

profile of v1, /device:TPU:0, one launch (start us, length us, event | category | flops | bytes accessed | tf_op | source)
XLA Modules:
  0.0 51.1 jit_solution(7845796093413375913)
XLA Ops:
  0.6 1.2 %copy.37 = bf16[25,2,4096]{2,0,1:T(8,128)(2,1)S(1)} copy(bf16[25,2,4096]{2,1,0:T(2,128)(2,1)} %param.9) | data formatting | bytes 819200 | tf_op args[1]
  1.9 0.0 copy-start.1
  1.9 1.0 %copy-done.1 = f32[16,2,4096]{2,1,0:T(2,128)S(1)} copy-done((f32[16,2,4096]{2,1,0:T(2,128)S(1)}, f32[16,2,4096]{2,1,0:T(2,128)}, u32[]{:S(2)}) %copy-start.1) | copy-done | bytes 524312
  2.9 0.0 copy-start.3
  2.9 0.0 copy-start.2
  2.9 0.3 copy.38
  3.2 0.0 copy-start
  3.2 0.3 copy-done.3
  3.6 0.1 cosine_multiply_fusion
  3.7 0.1 add.47
  3.8 0.1 add.48
  3.9 0.0 copy-done.2
  3.9 0.1 add.51
  4.0 0.1 copy.31
  4.1 0.0 copy-start.4
  4.1 0.6 %copy-done.4 = f32[64]{0:T(128)S(1)} copy-done((f32[64]{0:T(128)S(1)}, f32[64]{0:T(128)}, u32[]{:S(2)}) %copy-start.4) | copy-done | bytes 280
  4.7 0.0 copy-start.5
  4.7 0.7 %copy-done.5 = s32[16]{0:T(128)S(1)} copy-done((s32[16]{0:T(128)S(1)}, s32[16]{0:T(128)}, u32[]{:S(2)}) %copy-start.5) | copy-done | bytes 88
  5.4 0.2 select_reduce_fusion
  5.6 0.0 copy-start.6
  5.6 0.1 copy.32
  5.7 0.6 %copy-done.6 = s32[16]{0:T(128)S(1)} copy-done((s32[16]{0:T(128)S(1)}, s32[16]{0:T(128)}, u32[]{:S(2)}) %copy-start.6) | copy-done | bytes 88
  6.3 0.1 copy.33
  6.3 0.1 concatenate.3.ext_ref
  6.4 0.0 copy-done
  6.4 41.0 %shard_map.103 = (f32[2,32,512]{2,1,0:T(8,128)S(1)}, f32[8,128]{1,0:T(8,128)S(1)}) custom-call(f32[2,16,4096]{2,1,0:T(8,128)S(1)} %bitcast.16, bf16[2,32,4096]{2,1,0:T(8,128)(2,1)S(1)} %pad.8.tmpl_ref, f32[8,4096]{1,0:T(8,128)S(1)} %copy-done, f32[16,128]{1,0:T(8,128)S(1)} %concatenate.3.ext_ref), custom_call_target="tpu_custom_call" | custom-call | tf_op jit(solution)/shard_map/pallas_call | solution.py:474
  47.5 0.6 %dynamic-slice_bitcast_fusion = f32[25]{0:T(128)} fusion(f32[1,128]{1,0:T(1,128)S(1)} %slice.18, s32[]{:T(128)S(6)} %select_n.22), kind=kLoop, calls=%fused_computation.10 | loop fusion | bytes 204 | tf_op jit(solution)/shard_map/dynamic_slice | solution.py:506
  48.1 0.5 %slice.19 = f32[1,1]{1,0:T(1,128)} slice(f32[8,128]{1,0:T(8,128)S(1)} %get-tuple-element.6), slice={[1:2], [0:1]} | slice | bytes 8 | tf_op jit(solution)/shard_map/slice | solution.py:507
  49.2 0.7 %copy.34 = f32[25,2,512]{2,1,0:T(2,128)} copy(f32[25,2,512]{2,0,1:T(8,128)S(1)} %slice_bitcast_fusion) | data formatting | bytes 204800
  (12 shorter events, 0.1 us)
Async XLA Ops:
  1.9 1.0 %copy-start.1 = (f32[16,2,4096]{2,1,0:T(2,128)S(1)}, f32[16,2,4096]{2,1,0:T(2,128)}, u32[]{:S(2)}) copy-start(f32[16,2,4096]{2,1,0:T(2,128)} %param.8) | copy-start | bytes 1572868
  2.9 0.7 %copy-start.3 = (s32[16]{0:T(128)S(1)}, s32[16]{0:T(128)}, u32[]{:S(2)}) copy-start(s32[16]{0:T(128)} %param.13) | copy-start | bytes 196
  2.9 0.9 %copy-start.2 = (s32[9,2]{0,1:T(2,128)S(1)}, s32[9,2]{0,1:T(2,128)}, u32[]{:S(2)}) copy-start(s32[9,2]{0,1:T(2,128)} %param.10) | copy-start | bytes 220
  3.2 3.2 %copy-start = (f32[8,4096]{1,0:T(8,128)S(1)}, f32[8,4096]{1,0:T(8,128)}, u32[]{:S(2)}) copy-start(f32[8,4096]{1,0:T(8,128)} %constant.54.clone.wave_ref) | copy-start | bytes 393220
  4.1 0.7 %copy-start.4 = (f32[64]{0:T(128)S(1)}, f32[64]{0:T(128)}, u32[]{:S(2)}) copy-start(f32[64]{0:T(128)} %param.12) | copy-start | bytes 772
  4.7 0.7 %copy-start.5 = (s32[16]{0:T(128)S(1)}, s32[16]{0:T(128)}, u32[]{:S(2)}) copy-start(s32[16]{0:T(128)} %param.11) | copy-start | bytes 196
  5.6 0.7 %copy-start.6 = (s32[16]{0:T(128)S(1)}, s32[16]{0:T(128)}, u32[]{:S(2)}) copy-start(s32[16]{0:T(128)} %param.14) | copy-start | bytes 196

commit v2 on v1

--- a/solution.py
+++ b/solution.py
@@ -254,10 +254,10 @@
 
 
 def fused(
-    dims, part_ref, tmpl_ref, wave_ref, ext_ref, out_ref, small_ref,
-    held, images, corr, total, sib_out, sib_in, cls_out, cls_in, dom_out, dom_in, small_in,
-    own_sem, gather_s, gather_r, forward_s, forward_r, sib_s, sib_r, cls_s, cls_r,
-    dom_s, dom_r, small_s, small_r, small_a, small_b, small_c,
+    dims, part_hbm, tmpl_ref, wave_ref, micro_ref, noise_ref, prior_ref, label_ref, move_ref,
+    out_ref, weight_ref, evidence_ref, part_ref, held, images, corr, total, sib_out, sib_in, cls_out, cls_in, dom_out, dom_in, small_in,
+    own_sem, part_sem, gather_s, gather_r, forward_s, forward_r, sib_s, sib_r, cls_s, cls_r,
+    dom_s, dom_r, small_s, small_r, small_a, small_b, small_c, pair_s, pair_r,
 ):
     doms, clss, count, shifts, chunk = dims
     group, dom = lax.axis_index("groups"), lax.axis_index("dom")
@@ -281,21 +281,46 @@
         pl.semaphore_signal(barrier, inc=1, device_id=target, device_id_type=mesh_id)
     pl.semaphore_wait(barrier, clss + doms - 1)
 
-    pending = []
-    gathers = [
-        send(tmpl_ref.at[pix], held.at[pix, cls], gather_s.at[k], gather_r.at[k], target)
-        for k, target in enumerate(cls_peers)
-    ]
+    odd = lax.rem(dom, 2)
+    partner = (group, dom + 1 - 2 * odd, cls, pix)
+    features = RAD * ANG
+    part_size, common = 3 * features // 8, features // 4
+    own_lanes = pl.ds(pl.multiple_of(odd * part_size, ANG), part_size)
+    pair_lanes = pl.ds(pl.multiple_of((1 - odd) * part_size, ANG), part_size)
+    common_lanes = pl.ds(2 * part_size, common)
+    gathers = []
+    for n, lanes in enumerate((own_lanes, common_lanes)):
+        for k, target in enumerate(cls_peers):
+            gathers.append(
+                send(tmpl_ref.at[pix, :, lanes], held.at[pix, cls, :, lanes],
+                     gather_s.at[n, k], gather_r.at[n, k], target)
+            )
     own_copies = [
         pltpu.make_async_copy(tmpl_ref.at[c], held.at[c, cls], own_sem.at[c]) for c in range(2)
     ]
+    part_copy = pltpu.make_async_copy(part_hbm, part_ref, part_sem)
+    part_copy.start()
     for copy in own_copies:
         copy.start()
 
+    rows = lax.broadcasted_iota(jnp.int32, (count, ANG), 0)
+    noise = jnp.ones((count, ANG), jnp.float32)
+    prior = jnp.zeros((count, ANG), jnp.int32)
+    label = jnp.zeros((count, ANG), jnp.int32)
+    for i in range(count):
+        noise = jnp.where(rows == i, noise_ref[micro_ref[i]], noise)
+        prior = jnp.where(rows == i, prior_ref[i], prior)
+        label = jnp.where(rows == i, label_ref[i], label)
+    move_x = jnp.zeros((count, ANG), jnp.int32)
+    move_y = jnp.zeros((count, ANG), jnp.int32)
+    for t in range(shifts):
+        move_x = jnp.where(rows == t, move_ref[t, 0], move_x)
+        move_y = jnp.where(rows == t, move_ref[t, 1], move_y)
+    move_x, move_y = move_x.astype(jnp.float32), move_y.astype(jnp.float32)
+    part_copy.wait()
+
     step_size = ANG // ROT
     per_rot = shifts * count
-    move_x = ext_ref[:, 40:41] + jnp.zeros((count, ANG), jnp.float32)
-    move_y = ext_ref[:, 41:42] + jnp.zeros((count, ANG), jnp.float32)
 
     def make_images(g, carry):
         lanes = pl.ds(pl.multiple_of(g * ANG, ANG), ANG)
@@ -304,7 +329,7 @@
         cy, sy = powers(waves[2:3], waves[3:4], move_y)
         cosine = cx * cy - sx * sy
         sine_part = sx * cy + cx * sy
-        real, imag = part_ref[0, :, lanes], part_ref[1, :, lanes]
+        real, imag = part_ref[:, 0, lanes], part_ref[:, 1, lanes]
         for rot in range(ROT):
             if rot:
                 turn = ANG - rot * step_size
@@ -321,13 +346,24 @@
 
     lax.fori_loop(0, RAD, make_images, 0)
 
-    forwards = []
-    for k, copy in enumerate(gathers):
-        copy.wait_recv()
-        owner = lax.rem(cls + clss - 1 - k, clss)
-        forwards.append(
-            send(held.at[pix, owner], held.at[pix, owner], forward_s.at[k], forward_r.at[k], sibling)
-        )
+    owners = [lax.rem(cls + clss - 1 - k, clss) for k in range(clss - 1)]
+    forwards, pairs = [], []
+
+    def forward(n, k, lanes):
+        block = held.at[pix, owners[k], :, lanes]
+        forwards.append(send(block, block, forward_s.at[n, k], forward_r.at[n, k], sibling))
+
+    for k in range(clss - 1):
+        gathers[k].wait_recv()
+        block = held.at[pix, owners[k], :, own_lanes]
+        pairs.append(send(block, block, pair_s.at[k], pair_r.at[k], partner))
+        forward(0, k, own_lanes)
+    for k in range(clss - 1):
+        gathers[clss - 1 + k].wait_recv()
+        forward(1, k, common_lanes)
+    for k in range(clss - 1):
+        pairs[k].wait_recv()
+        forward(2, k, pair_lanes)
     for copy in own_copies:
         copy.wait()
 
@@ -350,21 +386,28 @@
         return step
 
     energy = jnp.zeros((clss * PAD, ANG), jnp.float32)
-    energy = lax.fori_loop(0, RAD * ANG // piece, correlate(pix), energy)
+    energy = lax.fori_loop(0, RAD * ANG // piece, correlate(pix), energy, unroll=True)
     for copy in forwards:
         copy.wait_recv()
-    energy = lax.fori_loop(0, RAD * ANG // piece, correlate(other), energy)
+    energy = lax.fori_loop(0, RAD * ANG // piece, correlate(other), energy, unroll=True)
     energy = jnp.sum(energy, axis=1, keepdims=True)
 
     turned = jnp.transpose(corr[...] - 0.5 * energy).reshape(ROT * shifts, count, clss * PAD)
     slot = lax.broadcasted_iota(jnp.int32, (count, clss * PAD), 1)
-    inverse = ext_ref[:, 0:1]
-    match = jnp.where(slot.astype(jnp.float32) == ext_ref[:, 1:2], PRIOR_REWARD, 0.0)
-    real_class = lax.rem(slot, PAD) < CLASS_COUNT // clss
+    inverse = 1.0 / noise
+    size_block = CLASS_COUNT // clss
+    real_class = lax.rem(slot, PAD) < size_block
+    class_index = lax.div(slot, PAD) * size_block + lax.rem(slot, PAD)
+    match = jnp.where(class_index == label, PRIOR_REWARD, 0.0)
     match = jnp.where(real_class, match, -1e30)
-    values = [
-        turned[n] * inverse + (match + ext_ref[:, 2 + n : 3 + n]) for n in range(ROT * shifts)
-    ]
+    values = []
+    for rot in range(ROT):
+        turn = lax.rem(rot + ROT - prior, ROT)
+        level = jnp.where(turn == 0, KAPPA, jnp.where(turn == 2, -KAPPA, 0.0)) + match
+        for t in range(shifts):
+            x, y = move_ref[t, 0], move_ref[t, 1]
+            move_prior = -MOVE_WEIGHT * (x * x + y * y).astype(jnp.float32)
+            values.append(turned[rot * shifts + t] * inverse + (level + move_prior))
     highest = functools.reduce(jnp.maximum, values)
     highest = jnp.max(highest, axis=1, keepdims=True)
     summed = functools.reduce(jnp.add, [jnp.exp(v - highest) for v in values])
@@ -439,14 +482,19 @@
             )
     for j in range(doms - 1):
         small_dom[j].wait_recv()
-    small_ref[...] = functools.reduce(
+    small = functools.reduce(
         jnp.add, [small_c[...]] + [small_in[clss + k] for k in range(doms - 1)]
     )
+    own_weights = functools.reduce(
+        jnp.add, [jnp.where(cls == k, small[0:1, k * PAD : (k + 1) * PAD], 0.0) for k in range(clss)]
+    )
+    weight_ref[...] = own_weights[:, :size_block]
+    evidence_ref[...] = small[1:2, 0:1] * (1.0 / (count * doms * clss * 2))
     for j in range(doms - 1):
         dom_copies[j].wait_recv()
         value = value + dom_in[j].astype(jnp.float32)
     out_ref[...] = value
-    for copy in gathers + forwards + sib_copies + sum(cls_copies, []) + dom_copies:
+    for copy in gathers + pairs + forwards + sib_copies + sum(cls_copies, []) + dom_copies:
         copy.wait_send()
     for copy in [small_sib] + small_cls + small_dom:
         copy.wait_send()
@@ -455,31 +503,23 @@
 def fused_body(doms, clss, particles, templates, offsets, micrograph, noise_var, prior_rot, earlier_class_labels):
     count, size_block, shifts = particles.shape[0], templates.shape[0], offsets.shape[0]
     chunk = RAD * ANG // (doms * 2)
-    inverse, turn_prior, _, move_prior = row_terms(
-        micrograph, prior_rot, earlier_class_labels, noise_var, offsets
-    )
-    slots = earlier_class_labels // size_block * PAD + earlier_class_labels % size_block
-    bias = (turn_prior.T[:, :, None] + move_prior[None, None, :]).reshape(count, ROT * shifts)
-    move = jnp.pad(offsets.astype(jnp.float32), ((0, count - shifts), (0, 0)))
-    ext = jnp.concatenate(
-        [inverse[:, None], slots.astype(jnp.float32)[:, None], bias,
-         jnp.zeros((count, 38 - ROT * shifts), jnp.float32), move,
-         jnp.zeros((count, ANG - 42), jnp.float32)], axis=1)
     tmpl = jnp.pad(jnp.transpose(templates, (1, 0, 2)), ((0, 0), (0, PAD - size_block), (0, 0)))
-    part = jnp.transpose(particles, (1, 0, 2))
     rows = ROT * shifts * count
     bf, f32 = jnp.bfloat16, jnp.float32
     dma = pltpu.SemaphoreType.DMA
     vmem = pl.BlockSpec(memory_space=pltpu.VMEM)
-    sums, small = pl.pallas_call(
+    smem = pl.BlockSpec(memory_space=pltpu.SMEM)
+    sums, weights, evidence = pl.pallas_call(
         functools.partial(fused, (doms, clss, count, shifts, chunk)),
         out_shape=[
             jax.ShapeDtypeStruct((2, PAD, chunk), f32),
-            jax.ShapeDtypeStruct((8, clss * PAD), f32),
+            jax.ShapeDtypeStruct((1, size_block), f32),
+            jax.ShapeDtypeStruct((1, 1), f32),
         ],
-        in_specs=[vmem] * 4,
-        out_specs=[vmem] * 2,
+        in_specs=[pl.BlockSpec(memory_space=pl.ANY), vmem, vmem] + [smem] * 5,
+        out_specs=[vmem] * 3,
         scratch_shapes=[
+            pltpu.VMEM(particles.shape, f32),
             pltpu.VMEM((2, clss, PAD, RAD * ANG), bf),
             pltpu.VMEM((2, rows, RAD * ANG), bf),
             pltpu.VMEM((clss * PAD, rows), f32),
@@ -491,21 +531,23 @@
             pltpu.VMEM((doms - 1, 2, PAD, chunk), bf),
             pltpu.VMEM((doms - 1, 2, PAD, chunk), bf),
             pltpu.VMEM((clss + doms - 1, 8, clss * PAD), f32),
-            dma((2,)), dma((clss - 1,)), dma((clss - 1,)), dma((clss - 1,)), dma((clss - 1,)),
+            dma((2,)), dma, dma((2, clss - 1)), dma((2, clss - 1)), dma((3, clss - 1)), dma((3, clss - 1)),
             dma((doms,)), dma((doms,)), dma((doms, clss - 1)), dma((doms, clss - 1)),
             dma((doms - 1,)), dma((doms - 1,)), dma((clss + doms - 1,)), dma((clss + doms - 1,)),
             pltpu.VMEM((8, clss * PAD), f32),
             pltpu.VMEM((8, clss * PAD), f32),
             pltpu.VMEM((8, clss * PAD), f32),
+            dma((clss - 1,)), dma((clss - 1,)),
         ],
         compiler_params=pltpu.CompilerParams(
             collective_id=0, has_side_effects=True, vmem_limit_bytes=44 * 2**20
         ),
-    )(part, tmpl, jnp.asarray(wave_tables()), ext)
+    )(
+        particles, tmpl, jnp.asarray(wave_tables()),
+        micrograph, noise_var, prior_rot, earlier_class_labels, offsets,
+    )
     class_sums = jnp.transpose(sums[:, :size_block], (1, 0, 2))
-    class_weights = lax.dynamic_slice(small[0], (lax.axis_index("cls") * PAD,), (size_block,))
-    log_evidence = small[1, :1] / (count * doms * clss * 2)
-    return class_sums, class_weights, log_evidence
+    return class_sums, weights.reshape(size_block), evidence.reshape(1)
 
 
 def solution(mesh):
@@ -521,6 +563,6 @@
     out_specs = (P(("groups", "cls"), None, ("dom", "pix")), P(("groups", "cls")), P("groups"))
     doms, clss = mesh.shape["dom"], mesh.shape["cls"]
     whole_radii = RAD % (doms * mesh.shape["pix"]) == 0
-    fits = mesh.shape["pix"] == 2 and doms > 1 and clss > 1 and clss * PAD <= ANG
+    fits = mesh.shape["pix"] == 2 and doms % 2 == 0 and clss > 1 and clss * PAD == ANG
     chosen = functools.partial(fused_body, doms, clss) if whole_radii and fits else body
     return jax.shard_map(chosen, mesh=mesh, in_specs=in_specs, out_specs=out_specs, check_vma=False)

time: 51.4 us -> 47.7 us (0.928)
  local copies, waits for them, and re-layouts: 7.23 us -> 3.88 us
    unnamed x17 -> x18, local copies, waits for them, and re-layouts: 5.47 us -> 3.83 us
    dynamic_slice x1 -> x0, local copies, waits for them, and re-layouts: 0.59 us -> none  [fused_body(): lax.dynamic_slice(small[0], (lax.axis_index('cls') * PAD,), (size_block,))]
    slice x2 -> x0, local copies, waits for them, and re-layouts: 0.52 us -> none  [the longest x1 0.51 us: fused_body(): log_evidence = small[1, :1] / (count * doms * clss * 2)]
where the time goes in v2:
time: 47.7 us; the launch traced here: 47.5 us
  Pallas kernels  41.2 us (86%)
  local copies, waits for them, and re-layouts  3.88 us (8%)
  between operations  2.38 us (5%)
    pallas_call x1, Pallas kernels, fused_body(): pl.pallas_call(functools.partial(fused, (doms, clss, count, shifts, chunk...  41.2 us
    unnamed x18, local copies, waits for them, and re-layouts  3.83 us

profile of v2, /device:TPU:0, one launch (start us, length us, event | category | flops | bytes accessed | tf_op | source)
XLA Modules:
  0.0 47.5 jit_solution(2360658123647189094)
XLA Ops:
  0.6 1.2 %copy.15 = bf16[25,2,4096]{2,0,1:T(8,128)(2,1)S(1)} copy(bf16[25,2,4096]{2,1,0:T(2,128)(2,1)} %param.9) | data formatting | bytes 819200 | tf_op args[1]
  1.9 0.0 copy-start.6
  1.9 0.0 copy-start
  1.9 0.0 copy-start.1
  2.0 0.6 %copy-done.6 = s32[9,2]{0,1:T(2,128)S(1)} copy-done((s32[9,2]{0,1:T(2,128)S(1)}, s32[9,2]{0,1:T(2,128)}, u32[]{:S(2)}) %copy-start.6) | copy-done | bytes 96
  2.6 0.0 copy-start.2
  2.6 0.0 copy-start.3
  2.6 0.0 copy-start.4
  2.6 0.0 copy-start.5
  2.6 0.1 copy.12.move_ref
  2.7 0.3 copy-done
  2.9 0.0 copy-done.1
  2.9 0.3 copy-done.2
  3.3 0.0 copy-done.3
  3.3 0.0 copy-done.4
  3.3 0.0 copy-done.5
  3.3 41.2 %shard_map.103 = (f32[2,32,512]{2,1,0:T(8,128)S(1)}, f32[1,25]{1,0:T(1,128)S(1)}, f32[1,1]{1,0:T(1,128)}) custom-call(f32[16,2,4096]{2,1,0:T(2,128)S(1)} %copy-done, bf16[2,32,4096]{2,1,0:T(8,128)(2,1)S(1)} %pad.4.tmpl_ref, f32[8,4096]{1,0:T(8,128)S(1)} %copy-done.1, s32[16]{0:T(128)S(1)} %copy-done.2, f32[64]{0:T(128)S(1)} %copy-done.3, s32[16]{0:T(128)S(1)} %copy-done.4, ...), custom_call_target="tpu_custom_call" | custom-call | tf_op jit(solution)/shard_map/pallas_call | solution.py:512
  44.6 0.7 %copy.13 = f32[25,2,512]{2,1,0:T(2,128)} copy(f32[25,2,512]{2,0,1:T(8,128)S(1)} %slice_bitcast_fusion) | data formatting | bytes 204800
  45.3 0.5 %copy.18 = f32[25]{0:T(128)} copy(f32[25]{0:T(128)S(1)} %bitcast.7) | data formatting | bytes 200
  (2 shorter events, 0.0 us)
Async XLA Ops:
  1.9 0.7 %copy-start.6 = (s32[9,2]{0,1:T(2,128)S(1)}, s32[9,2]{0,1:T(2,128)}, u32[]{:S(2)}) copy-start(s32[9,2]{0,1:T(2,128)} %param.10) | copy-start | bytes 220
  1.9 1.0 %copy-start = (f32[16,2,4096]{2,1,0:T(2,128)S(1)}, f32[16,2,4096]{2,1,0:T(2,128)}, u32[]{:S(2)}) copy-start(f32[16,2,4096]{2,1,0:T(2,128)} %part_hbm.1) | copy-start | bytes 1572868
  1.9 1.1 %copy-start.1 = (f32[8,4096]{1,0:T(8,128)S(1)}, f32[8,4096]{1,0:T(8,128)}, u32[]{:S(2)}) copy-start(f32[8,4096]{1,0:T(8,128)} %constant.5.clone.wave_ref) | copy-start | bytes 393220
  2.6 0.7 %copy-start.2 = (s32[16]{0:T(128)S(1)}, s32[16]{0:T(128)}, u32[]{:S(2)}) copy-start(s32[16]{0:T(128)} %micro_ref.1) | copy-start | bytes 196
  2.6 0.7 %copy-start.3 = (f32[64]{0:T(128)S(1)}, f32[64]{0:T(128)}, u32[]{:S(2)}) copy-start(f32[64]{0:T(128)} %noise_ref.1) | copy-start | bytes 772
  2.6 0.7 %copy-start.4 = (s32[16]{0:T(128)S(1)}, s32[16]{0:T(128)}, u32[]{:S(2)}) copy-start(s32[16]{0:T(128)} %prior_ref.1) | copy-start | bytes 196
  2.6 0.7 %copy-start.5 = (s32[16]{0:T(128)S(1)}, s32[16]{0:T(128)}, u32[]{:S(2)}) copy-start(s32[16]{0:T(128)} %label_ref.1) | copy-start | bytes 196

commit v3 on v2

--- a/solution.py
+++ b/solution.py
@@ -284,7 +284,7 @@
     odd = lax.rem(dom, 2)
     partner = (group, dom + 1 - 2 * odd, cls, pix)
     features = RAD * ANG
-    part_size, common = 3 * features // 8, features // 4
+    part_size, common = features // 8, 3 * features // 4
     own_lanes = pl.ds(pl.multiple_of(odd * part_size, ANG), part_size)
     pair_lanes = pl.ds(pl.multiple_of((1 - odd) * part_size, ANG), part_size)
     common_lanes = pl.ds(2 * part_size, common)

time: 47.7 us -> 45.3 us (0.950)
  Pallas kernels: 41.2 us -> 38.8 us
    pallas_call x1, Pallas kernels: 41.2 us -> 38.8 us  [fused_body(): pl.pallas_call(functools.partial(fused, (doms, clss, count, shifts, chunk...]
where the time goes in v3:
time: 45.3 us; the launch traced here: 45.1 us
  Pallas kernels  38.8 us (86%)
  local copies, waits for them, and re-layouts  3.88 us (9%)
  between operations  2.38 us (5%)
    pallas_call x1, Pallas kernels, fused_body(): pl.pallas_call(functools.partial(fused, (doms, clss, count, shifts, chunk...  38.8 us
    unnamed x18, local copies, waits for them, and re-layouts  3.83 us

profile of v3, /device:TPU:0, one launch (start us, length us, event | category | flops | bytes accessed | tf_op | source)
XLA Modules:
  0.0 45.1 jit_solution(3685193654652298301)
XLA Ops:
  0.6 1.2 %copy.15 = bf16[25,2,4096]{2,0,1:T(8,128)(2,1)S(1)} copy(bf16[25,2,4096]{2,1,0:T(2,128)(2,1)} %param.9) | data formatting | bytes 819200 | tf_op args[1]
  1.9 0.0 copy-start.6
  1.9 0.0 copy-start
  1.9 0.0 copy-start.1
  2.0 0.6 %copy-done.6 = s32[9,2]{0,1:T(2,128)S(1)} copy-done((s32[9,2]{0,1:T(2,128)S(1)}, s32[9,2]{0,1:T(2,128)}, u32[]{:S(2)}) %copy-start.6) | copy-done | bytes 96
  2.6 0.0 copy-start.2
  2.6 0.0 copy-start.3
  2.6 0.0 copy-start.4
  2.6 0.0 copy-start.5
  2.6 0.1 copy.12.move_ref
  2.7 0.3 copy-done
  2.9 0.0 copy-done.1
  2.9 0.3 copy-done.2
  3.3 0.0 copy-done.3
  3.3 0.0 copy-done.4
  3.3 0.0 copy-done.5
  3.3 38.8 %shard_map.103 = (f32[2,32,512]{2,1,0:T(8,128)S(1)}, f32[1,25]{1,0:T(1,128)S(1)}, f32[1,1]{1,0:T(1,128)}) custom-call(f32[16,2,4096]{2,1,0:T(2,128)S(1)} %copy-done, bf16[2,32,4096]{2,1,0:T(8,128)(2,1)S(1)} %pad.4.tmpl_ref, f32[8,4096]{1,0:T(8,128)S(1)} %copy-done.1, s32[16]{0:T(128)S(1)} %copy-done.2, f32[64]{0:T(128)S(1)} %copy-done.3, s32[16]{0:T(128)S(1)} %copy-done.4, ...), custom_call_target="tpu_custom_call" | custom-call | tf_op jit(solution)/shard_map/pallas_call | solution.py:512
  42.2 0.7 %copy.13 = f32[25,2,512]{2,1,0:T(2,128)} copy(f32[25,2,512]{2,0,1:T(8,128)S(1)} %slice_bitcast_fusion) | data formatting | bytes 204800
  42.9 0.5 %copy.18 = f32[25]{0:T(128)} copy(f32[25]{0:T(128)S(1)} %bitcast.7) | data formatting | bytes 200
  (2 shorter events, 0.0 us)
Async XLA Ops:
  1.9 0.7 %copy-start.6 = (s32[9,2]{0,1:T(2,128)S(1)}, s32[9,2]{0,1:T(2,128)}, u32[]{:S(2)}) copy-start(s32[9,2]{0,1:T(2,128)} %param.10) | copy-start | bytes 220
  1.9 1.0 %copy-start = (f32[16,2,4096]{2,1,0:T(2,128)S(1)}, f32[16,2,4096]{2,1,0:T(2,128)}, u32[]{:S(2)}) copy-start(f32[16,2,4096]{2,1,0:T(2,128)} %part_hbm.1) | copy-start | bytes 1572868
  1.9 1.1 %copy-start.1 = (f32[8,4096]{1,0:T(8,128)S(1)}, f32[8,4096]{1,0:T(8,128)}, u32[]{:S(2)}) copy-start(f32[8,4096]{1,0:T(8,128)} %constant.5.clone.wave_ref) | copy-start | bytes 393220
  2.6 0.7 %copy-start.2 = (s32[16]{0:T(128)S(1)}, s32[16]{0:T(128)}, u32[]{:S(2)}) copy-start(s32[16]{0:T(128)} %micro_ref.1) | copy-start | bytes 196
  2.6 0.7 %copy-start.3 = (f32[64]{0:T(128)S(1)}, f32[64]{0:T(128)}, u32[]{:S(2)}) copy-start(f32[64]{0:T(128)} %noise_ref.1) | copy-start | bytes 772
  2.6 0.7 %copy-start.4 = (s32[16]{0:T(128)S(1)}, s32[16]{0:T(128)}, u32[]{:S(2)}) copy-start(s32[16]{0:T(128)} %prior_ref.1) | copy-start | bytes 196
  2.6 0.7 %copy-start.5 = (s32[16]{0:T(128)S(1)}, s32[16]{0:T(128)}, u32[]{:S(2)}) copy-start(s32[16]{0:T(128)} %label_ref.1) | copy-start | bytes 196
